TPU v7x, 32 devices: a whole 2x2x4 slice. The times are simulated.
32 devices in a mesh: groups: 2 (over y), users: 4 (over z), hours: 4 (over x, core).
Axes of the slice: x: 2, y: 2, z: 4, core: 2. Of those that a mesh axis runs over, the one named last changes fastest.
Arguments:
- activity: bfloat16 [16384, 8192], P(('groups', 'users'), 'hours'), parts along dimension 0, may hold values from -6 to 6
- cohort: int32 [16384], P(('groups', 'users')), parts along dimension 0, may hold values from 0 to 15
- tap_table: float32 [16, 9], replicated, may hold values from 0.02 to 0.4
- sketch: bfloat16 [8192, 64], P('hours'), may hold values from -0.0625 to 0.0625
Outputs:
- basis: float32 [16384, 64], P(('groups', 'users', 'hours')), parts along dimension 0
- triangle: float32 [128, 64], P('groups'), parts along dimension 0
There are 2 independent parts, one for each index of `groups`. A program takes and returns all parts, laid end to end along the dimension named above; an argument that names none is the same for every part. Nothing has to cross between parts.
All inputs are finite; a program needn't handle non-finite values.
Results may differ from a plain program's by a relative error of at most 0.003.
Values may be sent and summed in bfloat16 or wider, within the bound.
A program may use at most 64 MiB of HBM per device.

v0:
```python
import math

import jax
import jax.numpy as jnp
from jax import lax
from jax.sharding import PartitionSpec as P

TAPS = 9


def with_halo(block, sides, width):
    for axis, dim in sides:
        count = lax.axis_size(axis)
        forward = [(i, i + 1) for i in range(count - 1)]
        backward = [(target, source) for source, target in forward]
        low = lax.ppermute(
            lax.slice_in_dim(block, block.shape[dim] - width, None, axis=dim), axis, forward
        )
        high = lax.ppermute(lax.slice_in_dim(block, 0, width, axis=dim), axis, backward)
        block = jnp.concatenate([low, block, high], axis=dim)
    return block


def partner_2(value, axis, distance):
    mask = 2**distance
    pairs = [(source, source ^ mask) for source in range(lax.axis_size(axis))]
    return lax.ppermute(value, axis, pairs)


def per_device(activity, cohort, tap_table, sketch):
    rows = activity.shape[0]
    width = activity.shape[1]
    reach = (TAPS - 1) // 2
    padded = with_halo(activity, (("hours", 1),), reach)
    onehot = (cohort[:, None] == jnp.arange(tap_table.shape[0], dtype=jnp.int32)[None, :]).astype(
        jnp.float32
    )
    taps = jnp.dot(onehot, tap_table, precision=lax.Precision.HIGHEST)
    share = rows // lax.axis_size("hours")
    total = jnp.zeros((rows, width), jnp.float32)
    for step in range(TAPS):
        total = total + taps[:, step : step + 1] * padded[:, step : step + width].astype(
            jnp.float32
        )
    smoothed = total.astype(jnp.bfloat16)
    summed = lax.psum(jnp.dot(smoothed, sketch, preferred_element_type=jnp.float32), "hours")
    local = lax.dynamic_slice_in_dim(summed, lax.axis_index("hours") * share, share, 0)
    gram = jnp.dot(local.T, local, precision=lax.Precision.HIGHEST)
    lower = jnp.linalg.cholesky(gram)
    levels = lax.axis_size(("users", "hours")).bit_length() - 1
    for level in range(levels):
        partner = partner_2(lower, ("users", "hours"), level)
        joined = jnp.dot(lower, lower.T, precision=lax.Precision.HIGHEST) + jnp.dot(
            partner, partner.T, precision=lax.Precision.HIGHEST
        )
        lower = jnp.linalg.cholesky(joined)
    basis = lax.linalg.triangular_solve(lower, local, left_side=False, lower=True, transpose_a=True)
    scale = 1.0 / math.sqrt(rows * lax.axis_size("users"))
    triangle = lower.T * jnp.float32(scale)
    return (basis, triangle)


def solution(mesh):
    return jax.shard_map(
        per_device,
        mesh=mesh,
        in_specs=(P(("groups", "users"), "hours"), P(("groups", "users")), P(), P("hours", None)),
        out_specs=(P(("groups", "users", "hours"), None), P("groups", None)),
        check_vma=False,
    )
```

profile of v0, /device:TPU:0, one launch (start us, length us, event | category | flops | bytes accessed | tf_op | source)
XLA Modules:
  0.0 174.9 jit_solution(3421940850101160094)
XLA Ops:
  7.2 1.5 fusion.27
  8.7 2.4 %collective-permute-start = (bf16[2048,4]{1,0:T(8,128)(2,1)S(1)}, bf16[2048,4]{1,0:T(8,128)(2,1)S(1)}, u32[]{:S(2)}, u32[]{:S(2)}) collective-permute-start(bf16[2048,4]{1,0:T(8,128)(2,1)S(1)} %get-tuple-element.6), channel_id=1, source_target_pairs={{0,1},{1,2},{2,3},{4,5},{5,6},{6,7},{8,9},{9,10},{10,11},{12,13},{... | collective-permute-start | bytes 49160 | tf_op jit(solution)/shard_map/ppermute | solution.py:16
  11.1 1.3 collective-permute-start.1
  12.4 8.3 %constant_dynamic-update-slice_fusion.1 = bf16[2048,2052]{1,0:T(8,128)(2,1)} fusion(bf16[2048,2048]{1,0:T(8,128)(2,1)} %param.5), kind=kLoop, calls=%fused_computation.51 | loop fusion | bytes 16777216
  20.7 0.9 fusion.4
  21.8 0.9 constant_dynamic-update-slice_fusion
  22.7 47.5 %fusion.3 = f32[2048,64]{0,1:T(8,128)} fusion(bf16[2048,64]{0,1:T(8,128)(2,1)S(1)} %copy-done, bf16[2048,2048]{1,0:T(8,128)(2,1)} %param.5, bf16[2048,4]{1,0:T(8,128)(2,1)S(1)} %collective-permute-done, bf16[2048,2052]{1,0:T(8,128)(2,1)} %constant_dynamic-update-slice_fusion, f32[2048]{0:T(1024)S(1)} %bitcast.55, f32[2048]{0:T(1024)S(1)} %bitcast.56, ...), kind=kOutput, calls=%fused_computation.9 | convolution fusion | flops 700448768 | bytes 42819584 | tf_op jit(solution)/shard_map/dot_general | solution.py:46
  70.2 37.9 %all-reduce.2.cloned.1.call-done = f32[2048,64]{0,1:T(8,128)} async-done(((f32[2048,64]{0,1:T(8,128)}), f32[2048,64]{0,1:T(8,128)}) %all-reduce.2.cloned.1.call-update) | async-done | bytes 524304 | tf_op jit(solution)/shard_map/psum | solution.py:46
  108.1 1.2 fusion.8
  109.4 5.8 %cholesky.89 = f32[64,64]{1,0:T(8,128)S(1)} custom-call(f32[64,64]{1,0:T(8,128)S(1)} %fusion.15), custom_call_target="Cholesky" | custom-call | tf_op jit(solution)/shard_map/jit(cholesky)/cholesky | solution.py:49
  115.3 0.6 compare_reduce_fusion.4
  115.9 0.7 select_select_fusion.4
  116.9 1.0 collective-permute-done.2
  118.2 5.8 %cholesky.100 = f32[64,64]{1,0:T(8,128)S(1)} custom-call(f32[64,64]{1,0:T(8,128)S(1)} %fusion.14), custom_call_target="Cholesky" | custom-call | tf_op jit(solution)/shard_map/jit(cholesky)/cholesky | solution.py:56
  124.7 0.7 select_select_fusion.3
  125.7 3.6 %collective-permute-done.3 = f32[64,64]{1,0:T(8,128)S(1)} collective-permute-done((f32[64,64]{1,0:T(8,128)S(1)}, f32[64,64]{1,0:T(8,128)S(1)}, u32[]{:S(2)}, u32[]{:S(2)}) %collective-permute-start.3) | collective-permute-done | bytes 16416 | tf_op jit(solution)/shard_map/ppermute | solution.py:27
  129.6 5.8 %cholesky.111 = f32[64,64]{1,0:T(8,128)S(1)} custom-call(f32[64,64]{1,0:T(8,128)S(1)} %fusion.13), custom_call_target="Cholesky" | custom-call | tf_op jit(solution)/shard_map/jit(cholesky)/cholesky | solution.py:56
  135.5 0.6 compare_reduce_fusion.2
  136.1 0.7 select_select_fusion.2
  136.8 1.5 collective-permute-start.4
  138.5 2.2 %collective-permute-done.4 = f32[64,64]{1,0:T(8,128)S(1)} collective-permute-done((f32[64,64]{1,0:T(8,128)S(1)}, f32[64,64]{1,0:T(8,128)S(1)}, u32[]{:S(2)}, u32[]{:S(2)}) %collective-permute-start.4) | collective-permute-done | bytes 16416 | tf_op jit(solution)/shard_map/ppermute | solution.py:27
  141.1 5.8 %cholesky.122 = f32[64,64]{1,0:T(8,128)S(1)} custom-call(f32[64,64]{1,0:T(8,128)S(1)} %fusion.12), custom_call_target="Cholesky" | custom-call | tf_op jit(solution)/shard_map/jit(cholesky)/cholesky | solution.py:56
  147.0 0.6 compare_reduce_fusion.1
  147.6 0.7 select_select_fusion.1
  148.3 2.5 %collective-permute-start.5 = (f32[64,64]{1,0:T(8,128)S(1)}, f32[64,64]{1,0:T(8,128)S(1)}, u32[]{:S(2)}, u32[]{:S(2)}) collective-permute-start(f32[64,64]{1,0:T(8,128)S(1)} %select_select_fusion.1), channel_id=1, source_target_pairs={{0,8},{1,9},{2,10},{3,11},{4,12},{5,13},{6,14},{7,15},{8,0},{9,1},... | collective-permute-start | bytes 49160 | tf_op jit(solution)/shard_map/ppermute | solution.py:27
  150.9 2.2 %collective-permute-done.5 = f32[64,64]{1,0:T(8,128)S(1)} collective-permute-done((f32[64,64]{1,0:T(8,128)S(1)}, f32[64,64]{1,0:T(8,128)S(1)}, u32[]{:S(2)}, u32[]{:S(2)}) %collective-permute-start.5) | collective-permute-done | bytes 16416 | tf_op jit(solution)/shard_map/ppermute | solution.py:27
  153.4 5.8 %cholesky.133 = f32[64,64]{1,0:T(8,128)S(1)} custom-call(f32[64,64]{1,0:T(8,128)S(1)} %fusion.11), custom_call_target="Cholesky" | custom-call | tf_op jit(solution)/shard_map/jit(cholesky)/cholesky | solution.py:56
  159.3 0.6 compare_reduce_fusion
  160.0 0.7 multiply_bitcast_fusion
  160.6 4.9 %custom-call.5 = f32[1,64,64]{1,2,0:T(8,128)S(1)} custom-call(f32[1,64,64]{2,1,0:T(8,128)S(1)} %get-tuple-element.17), custom_call_target="InvertDiagBlocksLowerTriangular" | custom-call | tf_op jit(solution)/shard_map/triangular_solve | solution.py:57
  165.5 0.7 copy.19
  166.2 1.9 %fusion.6 = f32[512,64]{0,1:T(8,128)} fusion(f32[2048,64]{0,1:T(8,128)} %all-reduce.2.cloned.1.call-done, s32[]{:T(128)S(6)} %select_n.6, f32[1,64,64]{1,2,0:T(8,128)S(1)} %custom-call.5), kind=kOutput, calls=%fused_computation.17 | convolution fusion | flops 25165824 | bytes 278532 | tf_op jit(solution)/shard_map/triangular_solve | solution.py:57
  (37 shorter events, 3.1 us)
Async XLA Ops:
  7.2 15.5 %copy-start = (bf16[2048,64]{0,1:T(8,128)(2,1)S(1)}, bf16[2048,64]{0,1:T(8,128)(2,1)}, u32[]{:S(2)}) copy-start(bf16[2048,64]{0,1:T(8,128)(2,1)} %param.8) | copy-start | bytes 786436
  7.2 100.9 %all-reduce.2.cloned.1.call-start = ((), (), s32[]{:S(2)}) async-start(), calls=%async_computation | async-start | bytes 1048576 | tf_op jit(solution)/shard_map/psum | solution.py:46
  8.7 12.1 %copy-start.1 = (f32[16,9]{1,0:T(8,128)S(1)}, f32[16,9]{1,0:T(8,128)}, u32[]{:S(2)}) copy-start(f32[16,9]{1,0:T(8,128)} %param.7) | copy-start | bytes 1732
  8.7 12.1 %copy-start.2 = (s32[2048]{0:T(1024)S(1)}, s32[2048]{0:T(1024)}, u32[]{:S(2)}) copy-start(s32[2048]{0:T(1024)} %param.6) | copy-start | bytes 24580
  8.7 14.0 %collective-permute-start = (bf16[2048,4]{1,0:T(8,128)(2,1)S(1)}, bf16[2048,4]{1,0:T(8,128)(2,1)S(1)}, u32[]{:S(2)}, u32[]{:S(2)}) collective-permute-start(bf16[2048,4]{1,0:T(8,128)(2,1)S(1)} %get-tuple-element.6), channel_id=1, source_target_pairs={{0,1},{1,2},{2,3},{4,5},{5,6},{6,7},{8,9},{9,10},{10,11},{12,13},{... | collective-permute-start | bytes 49160 | tf_op jit(solution)/shard_map/ppermute | solution.py:16
  11.1 10.7 %collective-permute-start.1 = (bf16[2048,4]{1,0:T(8,128)(2,1)S(1)}, bf16[2048,4]{1,0:T(8,128)(2,1)S(1)}, u32[]{:S(2)}, u32[]{:S(2)}) collective-permute-start(bf16[2048,4]{1,0:T(8,128)(2,1)S(1)} %get-tuple-element.5), channel_id=1, source_target_pairs={{1,0},{2,1},{3,2},{5,4},{6,5},{7,6},{9,8},{10,9},{11,10},{13,12},{... | collective-permute-start | bytes 49160 | tf_op jit(solution)/shard_map/ppermute | solution.py:19
  116.6 1.3 collective-permute-start.2
  125.4 4.0 %collective-permute-start.3 = (f32[64,64]{1,0:T(8,128)S(1)}, f32[64,64]{1,0:T(8,128)S(1)}, u32[]{:S(2)}, u32[]{:S(2)}) collective-permute-start(f32[64,64]{1,0:T(8,128)S(1)} %select_select_fusion.3), channel_id=1, source_target_pairs={{0,2},{1,3},{2,0},{3,1},{4,6},{5,7},{6,4},{7,5},{8,10},{9,11},{10,... | collective-permute-start | bytes 49160 | tf_op jit(solution)/shard_map/ppermute | solution.py:27
  136.8 4.0 %collective-permute-start.4 = (f32[64,64]{1,0:T(8,128)S(1)}, f32[64,64]{1,0:T(8,128)S(1)}, u32[]{:S(2)}, u32[]{:S(2)}) collective-permute-start(f32[64,64]{1,0:T(8,128)S(1)} %select_select_fusion.2), channel_id=1, source_target_pairs={{0,4},{1,5},{2,6},{3,7},{4,0},{5,1},{6,2},{7,3},{8,12},{9,13},{10,... | collective-permute-start | bytes 49160 | tf_op jit(solution)/shard_map/ppermute | solution.py:27
  148.3 4.9 %collective-permute-start.5 = (f32[64,64]{1,0:T(8,128)S(1)}, f32[64,64]{1,0:T(8,128)S(1)}, u32[]{:S(2)}, u32[]{:S(2)}) collective-permute-start(f32[64,64]{1,0:T(8,128)S(1)} %select_select_fusion.1), channel_id=1, source_target_pairs={{0,8},{1,9},{2,10},{3,11},{4,12},{5,13},{6,14},{7,15},{8,0},{9,1},... | collective-permute-start | bytes 49160 | tf_op jit(solution)/shard_map/ppermute | solution.py:27
Sparse Core Ops, SparseCore 0:
  70.3 37.7 all-reduce.1
where the time goes:
time: 175 us
  matrix products  53 us (30%)
  waiting for transfers between devices  47 us (27%)
  other arithmetic  40.8 us (23%)
  between operations  14.3 us (8%)
  local copies, waits for them, and re-layouts  11.9 us (7%)
  starting transfers between devices  8 us (5%)
    dot_general x1, matrix products, per_device(): jnp.dot(smoothed, sketch, preferred_element_type=jnp.float32)  47.5 us
    psum x1, waiting for transfers between devices, per_device(): lax.psum(jnp.dot(smoothed, sketch, preferred_element_type=jnp.float32), '...  37.9 us
    another operation x12, other arithmetic, per_device(): lower = jnp.linalg.cholesky(joined)  26.1 us
    unnamed x8, local copies, waits for them, and re-layouts  9.07 us
    ppermute x4, waiting for transfers between devices, partner_2(): return lax.ppermute(value, axis, pairs)  9.06 us
    another operation x3, other arithmetic, per_device(): lower = jnp.linalg.cholesky(gram)  6.52 us
    another operation x1, other arithmetic, per_device(): lax.linalg.triangular_solve(lower, local, left_side=False, lower=True, tr...  4.9 us
    ppermute x4, starting transfers between devices, partner_2(): return lax.ppermute(value, axis, pairs)  4.28 us
  transfers between devices with their start and end apart: 7, of which 5 were waited for; matrix products, arithmetic and copies ran while one was open for 6% of the time, Pallas kernels for 0%

commit v1 on v0

v1 whole, which is shorter than its diff:
```python
import functools
import math

import jax
import jax.numpy as jnp
from jax import lax
from jax.experimental import pallas as pl
from jax.experimental.pallas import tpu as pltpu
from jax.sharding import PartitionSpec as P

TAPS = 9
REACH = (TAPS - 1) // 2
EDGE = 128
HIGHEST = lax.Precision.HIGHEST
MESH = pl.DeviceIdType.MESH


def flip(index, mask):
    bit = 1
    while bit <= mask:
        if mask & bit:
            index = index + bit - 2 * bit * ((index // bit) % 2)
        bit *= 2
    return index


def dot_nt(a, b, precision=None):
    return lax.dot_general(
        a, b, (((1,), (1,)), ((), ())), precision=precision, preferred_element_type=jnp.float32
    )


def eliminate(gram):
    k = gram.shape[0]
    row_id = lax.broadcasted_iota(jnp.int32, (k, 2 * k), 0)
    lane_id = lax.broadcasted_iota(jnp.int32, (k, 2 * k), 1)
    eye = (row_id[:, :k] == lane_id[:, :k]).astype(jnp.float32)
    work = jnp.concatenate([gram, eye], axis=1)
    for step in range(k - 1):
        row = work[step : step + 1, :]
        scaled = row / work[step : step + 1, step : step + 1]
        col = jnp.where(row_id > step, work[:, step : step + 1], 0.0)
        work = work - col * scaled
    diag = jnp.sum(jnp.where(row_id == lane_id, work, 0.0), axis=1, keepdims=True)
    work = work * lax.rsqrt(diag)
    upper = jnp.where(row_id[:, :k] <= lane_id[:, :k], work[:, :k], 0.0)
    inverse = jnp.where(row_id[:, :k] >= lane_id[:, :k], work[:, k:], 0.0)
    return upper, inverse


def pack(square):
    half = square.shape[0] // 2
    return jnp.concatenate([square[:half], square[half:]], axis=1)


def unpack(packed):
    k = packed.shape[1] // 2
    return jnp.concatenate([packed[:, :k], packed[:, k:]], axis=0)


def kernel(
    n_users, n_hours, activity, cohort, table, sketch, basis, triangle,
    block, edge, shifted, taps, send, recv, gram_h, gram_u,
    load_sem, edge_send, edge_recv, part_send, part_recv, gh_send, gh_recv, gu_send, gu_recv,
):
    users = lax.axis_index("users")
    hours = lax.axis_index("hours")
    rows, width = activity.shape
    k = sketch.shape[0]
    share = rows // n_hours

    order = list(range(n_hours - 1, 0, -1)) + [0]
    loads = []
    for mask in order:
        start = pl.multiple_of(flip(hours, mask) * share, share)
        load = pltpu.make_async_copy(
            activity.at[pl.ds(start, share), :], block.at[mask], load_sem.at[mask]
        )
        load.start()
        loads.append(load)

    barrier = pltpu.get_barrier_semaphore()
    for mask in range(1, n_hours):
        pl.semaphore_signal(
            barrier, inc=1, device_id={"hours": flip(hours, mask)}, device_id_type=MESH
        )
    for step in range(1, n_users):
        pl.semaphore_signal(
            barrier, inc=1, device_id={"users": (users + step) % n_users}, device_id_type=MESH
        )
    pl.semaphore_wait(barrier, n_hours - 1 + n_users - 1)

    to_right = pltpu.make_async_remote_copy(
        src_ref=sketch.at[:, pl.ds(width - EDGE, EDGE)],
        dst_ref=edge.at[0],
        send_sem=edge_send.at[0],
        recv_sem=edge_recv.at[0],
        device_id={"hours": (hours + 1) % n_hours},
        device_id_type=MESH,
    )
    to_left = pltpu.make_async_remote_copy(
        src_ref=sketch.at[:, pl.ds(0, EDGE)],
        dst_ref=edge.at[1],
        send_sem=edge_send.at[1],
        recv_sem=edge_recv.at[1],
        device_id={"hours": (hours + n_hours - 1) % n_hours},
        device_id_type=MESH,
    )
    to_right.start()
    to_left.start()

    cohorts = table.shape[0]
    onehot = (
        lax.broadcasted_iota(jnp.int32, (cohorts, rows), 0) == cohort[...]
    ).astype(jnp.float32)
    taps[...] = lax.dot_general(
        table[...], onehot, (((0,), (0,)), ((), ())),
        precision=HIGHEST, preferred_element_type=jnp.float32,
    )

    to_right.wait()
    to_left.wait()
    low = edge[0].astype(jnp.float32)
    high = edge[1].astype(jnp.float32)
    turned = jnp.concatenate(
        [
            jnp.where(hours > 0, low, jnp.zeros_like(low)),
            sketch[...].astype(jnp.float32),
            jnp.where(hours < n_hours - 1, high, jnp.zeros_like(high)),
        ],
        axis=1,
    )
    for step in range(TAPS):
        shift = (step - REACH) % turned.shape[1]
        moved = turned if shift == 0 else pltpu.roll(turned, shift, 1)
        shifted[pl.ds(step * k, k), :] = moved[:, EDGE : EDGE + width].astype(jnp.bfloat16)

    parts = []
    local = None
    for load, mask in zip(loads, order):
        load.wait()
        start = pl.multiple_of(flip(hours, mask) * share, share)
        product = dot_nt(shifted[...], block[mask])
        total = taps[pl.ds(0, 1), pl.ds(start, share)] * product[:k]
        for step in range(1, TAPS):
            total += (
                taps[pl.ds(step, 1), pl.ds(start, share)] * product[step * k : (step + 1) * k]
            )
        if mask:
            send[mask - 1] = total
            copy = pltpu.make_async_remote_copy(
                src_ref=send.at[mask - 1],
                dst_ref=recv.at[mask - 1],
                send_sem=part_send.at[mask - 1],
                recv_sem=part_recv.at[mask - 1],
                device_id={"hours": flip(hours, mask)},
                device_id_type=MESH,
            )
            copy.start()
            parts.append((copy, mask))
        else:
            local = total
    for copy, mask in reversed(parts):
        copy.wait()
        local = local + recv[mask - 1]

    gram = pack(dot_nt(local, local, HIGHEST))
    for axis, count, me, slots, send_sems, recv_sems in (
        ("hours", n_hours, hours, gram_h, gh_send, gh_recv),
        ("users", n_users, users, gram_u, gu_send, gu_recv),
    ):
        slots[me] = gram
        copies = []
        for step in range(1, count):
            copy = pltpu.make_async_remote_copy(
                src_ref=slots.at[me],
                dst_ref=slots.at[me],
                send_sem=send_sems.at[step - 1],
                recv_sem=recv_sems.at[step - 1],
                device_id={axis: (me + step) % count},
                device_id_type=MESH,
            )
            copy.start()
            copies.append(copy)
        for copy in copies:
            copy.wait()
        gram = slots[0]
        for slot in range(1, count):
            gram = gram + slots[slot]

    upper, inverse = eliminate(unpack(gram))
    triangle[...] = upper * (1.0 / math.sqrt(rows * n_users))
    basis[...] = jnp.dot(
        inverse, local, precision=HIGHEST, preferred_element_type=jnp.float32
    )


def per_device(activity, cohort, tap_table, sketch):
    n_users, n_hours = lax.axis_size("users"), lax.axis_size("hours")
    rows, width = activity.shape
    k = sketch.shape[1]
    share = rows // n_hours
    dma = lambda count: pltpu.SemaphoreType.DMA((count,))
    vmem = pl.BlockSpec(memory_space=pltpu.VMEM)
    basis, triangle = pl.pallas_call(
        functools.partial(kernel, n_users, n_hours),
        out_shape=(
            jax.ShapeDtypeStruct((k, share), jnp.float32),
            jax.ShapeDtypeStruct((k, k), jnp.float32),
        ),
        in_specs=[pl.BlockSpec(memory_space=pl.ANY), vmem, vmem, vmem],
        out_specs=(vmem, vmem),
        scratch_shapes=[
            pltpu.VMEM((n_hours, share, width), jnp.bfloat16),
            pltpu.VMEM((2, k, EDGE), jnp.bfloat16),
            pltpu.VMEM((TAPS * k, width), jnp.bfloat16),
            pltpu.VMEM((TAPS, rows), jnp.float32),
            pltpu.VMEM((n_hours - 1, k, share), jnp.float32),
            pltpu.VMEM((n_hours - 1, k, share), jnp.float32),
            pltpu.VMEM((n_hours, k // 2, 2 * k), jnp.float32),
            pltpu.VMEM((n_users, k // 2, 2 * k), jnp.float32),
            dma(n_hours), dma(2), dma(2),
            dma(n_hours - 1), dma(n_hours - 1),
            dma(n_hours - 1), dma(n_hours - 1),
            dma(n_users - 1), dma(n_users - 1),
        ],
        compiler_params=pltpu.CompilerParams(
            collective_id=0, has_side_effects=True, vmem_limit_bytes=56 * 1024 * 1024
        ),
        name="range_finder",
    )(activity, cohort[None, :], tap_table, sketch.T)
    return basis.T, triangle


def solution(mesh):
    return jax.shard_map(
        per_device,
        mesh=mesh,
        in_specs=(P(("groups", "users"), "hours"), P(("groups", "users")), P(), P("hours", None)),
        out_specs=(P(("groups", "users", "hours"), None), P("groups", None)),
        check_vma=False,
    )
```

time: 175 us -> 34.5 us (0.20)
  matrix products: 53 us -> 0 us
  waiting for transfers between devices: 47 us -> 0 us
  other arithmetic: 40.8 us -> 0 us
  Pallas kernels: 0 us -> 30.7 us
  between operations: 14.3 us -> 0.64 us
  local copies, waits for them, and re-layouts: 11.9 us -> 2.94 us
  starting transfers between devices: 8 us -> 0 us
    dot_general x11 -> x0, matrix products: 51.1 us -> none  [the longest x1 47.5 us: per_device(): jnp.dot(smoothed, sketch, preferred_element_type=jnp.float32)]
    psum x1 -> x0, waiting for transfers between devices: 37.9 us -> none  [per_device(): lax.psum(jnp.dot(smoothed, sketch, preferred_element_type=jnp.float32), '...]
    another operation x16 -> x0, other arithmetic: 37.5 us -> none  [the longest x12 26.1 us: per_device(): lower = jnp.linalg.cholesky(joined)]
    pallas_call x0 -> x1, Pallas kernels: none -> 30.7 us  [per_device(): pl.pallas_call(functools.partial(kernel, n_users, n_hours), out_shape=(ja...]
    ppermute x6 -> x0, waiting for transfers between devices: 9.07 us -> none  [the longest x4 9.06 us: partner_2(): return lax.ppermute(value, axis, pairs)]
    ppermute x6 -> x0, starting transfers between devices: 7.96 us -> none  [the longest x4 4.28 us: partner_2(): return lax.ppermute(value, axis, pairs)]
    unnamed x8 -> x2, local copies, waits for them, and re-layouts: 9.07 us -> 2.94 us
    select_n x4 -> x0, other arithmetic: 2.61 us -> none  [the longest x3 1.95 us: per_device(): lower = jnp.linalg.cholesky(joined)]
  transfers between devices with their start and end apart: 7 -> 0, of which waited for: 5 -> 0; matrix products, arithmetic and copies ran while one was open for 6% -> 0% of each run, Pallas kernels for 0% -> 0%
where the time goes in v1:
time: 34.5 us; the launch traced here: 34.3 us
  Pallas kernels  30.7 us (89%)
  local copies, waits for them, and re-layouts  2.94 us (9%)
  between operations  0.64 us (2%)
    pallas_call x1, Pallas kernels, per_device(): pl.pallas_call(functools.partial(kernel, n_users, n_hours), out_shape=(ja...  30.7 us
    unnamed x2, local copies, waits for them, and re-layouts  2.94 us

profile of v1, /device:TPU:0, one launch (start us, length us, event | category | flops | bytes accessed | tf_op | source)
XLA Modules:
  0.0 34.3 jit_solution(18335759904781647530)
XLA Ops:
  0.6 30.7 %range_finder.1 = (f32[64,512]{1,0:T(8,128)}, f32[64,64]{1,0:T(8,128)}) custom-call(bf16[2048,2048]{1,0:T(8,128)(2,1)} %activity.1, s32[1,2048]{1,0:T(1,128)} %bitcast.5, f32[16,9]{1,0:T(8,128)} %table.1, bf16[64,2048]{1,0:T(8,128)(2,1)} %bitcast.3), custom_call_target="tpu_custom_call" | custom-call | tf_op jit(solution)/shard_map/range_finder/pallas_call | solution.py:205
  31.3 1.6 %copy.8 = f32[512,64]{0,1:T(8,128)} copy(f32[512,64]{0,1:T(8,128)} %bitcast.4) | data formatting | bytes 262144
  32.9 1.4 %copy.9 = f32[64,64]{1,0:T(8,128)} copy(f32[64,64]{1,0:T(8,128)} %get-tuple-element.9) | data formatting | bytes 32768

commit v2 on v1

--- a/solution.py
+++ b/solution.py
@@ -11,6 +11,7 @@
 TAPS = 9
 REACH = (TAPS - 1) // 2
 EDGE = 128
+PANEL = 8
 HIGHEST = lax.Precision.HIGHEST
 MESH = pl.DeviceIdType.MESH
 
@@ -36,13 +37,26 @@
     lane_id = lax.broadcasted_iota(jnp.int32, (k, 2 * k), 1)
     eye = (row_id[:, :k] == lane_id[:, :k]).astype(jnp.float32)
     work = jnp.concatenate([gram, eye], axis=1)
-    for step in range(k - 1):
-        row = work[step : step + 1, :]
-        scaled = row / work[step : step + 1, step : step + 1]
-        col = jnp.where(row_id > step, work[:, step : step + 1], 0.0)
-        work = work - col * scaled
-    diag = jnp.sum(jnp.where(row_id == lane_id, work, 0.0), axis=1, keepdims=True)
-    work = work * lax.rsqrt(diag)
+    diag_id = lax.broadcasted_iota(jnp.int32, (PANEL, 2 * k), 0)
+    done = []
+    for first in range(0, k, PANEL):
+        rows = work.shape[0]
+        below = lax.broadcasted_iota(jnp.int32, (rows, 2 * k), 0)
+        cols = [
+            jnp.broadcast_to(work[:, first + i : first + i + 1], (rows, 2 * k))
+            for i in range(PANEL)
+        ]
+        pivots = jnp.zeros((PANEL, 2 * k), jnp.float32)
+        for i in range(PANEL):
+            pivot = cols[i][i : i + 1, :]
+            pivots = jnp.where(diag_id == i, pivot, pivots)
+            col = jnp.where(below > i, cols[i], 0.0) * (1.0 / pivot)
+            for later in range(i + 1, PANEL):
+                cols[later] = cols[later] - col * cols[i][later : later + 1, :]
+            work = work - col * work[i : i + 1, :]
+        done.append(work[:PANEL] * lax.rsqrt(pivots))
+        work = work[PANEL:]
+    work = jnp.concatenate(done, axis=0)
     upper = jnp.where(row_id[:, :k] <= lane_id[:, :k], work[:, :k], 0.0)
     inverse = jnp.where(row_id[:, :k] >= lane_id[:, :k], work[:, k:], 0.0)
     return upper, inverse
@@ -59,8 +73,8 @@
 
 
 def kernel(
-    n_users, n_hours, activity, cohort, table, sketch, basis, triangle,
-    block, edge, shifted, taps, send, recv, gram_h, gram_u,
+    n_users, n_hours, activity, cohort, table, sketch, local_out, gram_out,
+    block, edge, shifted, ends, taps, send, recv, gram_h, gram_u,
     load_sem, edge_send, edge_recv, part_send, part_recv, gh_send, gh_recv, gu_send, gu_recv,
 ):
     users = lax.axis_index("users")
@@ -118,51 +132,62 @@
         precision=HIGHEST, preferred_element_type=jnp.float32,
     )
 
-    to_right.wait()
-    to_left.wait()
-    low = edge[0].astype(jnp.float32)
-    high = edge[1].astype(jnp.float32)
-    turned = jnp.concatenate(
-        [
-            jnp.where(hours > 0, low, jnp.zeros_like(low)),
-            sketch[...].astype(jnp.float32),
-            jnp.where(hours < n_hours - 1, high, jnp.zeros_like(high)),
-        ],
-        axis=1,
-    )
+    middle = sketch[...].astype(jnp.float32)
+    blank = jnp.zeros((k, EDGE), jnp.float32)
+    turned = jnp.concatenate([blank, middle, blank], axis=1)
     for step in range(TAPS):
         shift = (step - REACH) % turned.shape[1]
         moved = turned if shift == 0 else pltpu.roll(turned, shift, 1)
         shifted[pl.ds(step * k, k), :] = moved[:, EDGE : EDGE + width].astype(jnp.bfloat16)
 
-    parts = []
-    local = None
+    loads[0].wait()
+    product = dot_nt(shifted[...], block[order[0]])
+
+    to_right.wait()
+    to_left.wait()
+    low = jnp.where(hours > 0, edge[0].astype(jnp.float32), blank)
+    high = jnp.where(hours < n_hours - 1, edge[1].astype(jnp.float32), blank)
+    turned = jnp.concatenate([low, blank, blank, high], axis=1)
+    for step in range(TAPS):
+        shift = (step - REACH) % turned.shape[1]
+        moved = turned if shift == 0 else pltpu.roll(turned, shift, 1)
+        ends[pl.ds(step * k, k), :] = moved[:, EDGE : 3 * EDGE].astype(jnp.bfloat16)
+    shifted[:, pl.ds(0, EDGE)] += ends[:, pl.ds(0, EDGE)]
+    shifted[:, pl.ds(width - EDGE, EDGE)] += ends[:, pl.ds(EDGE, EDGE)]
+    outer = jnp.concatenate(
+        [block[order[0], :, pl.ds(0, EDGE)], block[order[0], :, pl.ds(width - EDGE, EDGE)]], axis=1
+    )
+    product += dot_nt(ends[...], outer)
+
+    copies = {}
     for load, mask in zip(loads, order):
-        load.wait()
         start = pl.multiple_of(flip(hours, mask) * share, share)
-        product = dot_nt(shifted[...], block[mask])
+        if mask != order[0]:
+            load.wait()
+            product = dot_nt(shifted[...], block[mask])
         total = taps[pl.ds(0, 1), pl.ds(start, share)] * product[:k]
         for step in range(1, TAPS):
             total += (
                 taps[pl.ds(step, 1), pl.ds(start, share)] * product[step * k : (step + 1) * k]
             )
+        bit = 1
+        while mask + bit < n_hours and (mask == 0 or bit < mask & -mask):
+            copies[mask + bit].wait()
+            total += recv[mask + bit - 1]
+            bit *= 2
         if mask:
             send[mask - 1] = total
-            copy = pltpu.make_async_remote_copy(
+            copies[mask] = pltpu.make_async_remote_copy(
                 src_ref=send.at[mask - 1],
                 dst_ref=recv.at[mask - 1],
                 send_sem=part_send.at[mask - 1],
                 recv_sem=part_recv.at[mask - 1],
-                device_id={"hours": flip(hours, mask)},
+                device_id={"hours": flip(hours, mask & -mask)},
                 device_id_type=MESH,
             )
-            copy.start()
-            parts.append((copy, mask))
-        else:
-            local = total
-    for copy, mask in reversed(parts):
-        copy.wait()
-        local = local + recv[mask - 1]
+            copies[mask].start()
+    local = total
+    local_out[...] = local
 
     gram = pack(dot_nt(local, local, HIGHEST))
     for axis, count, me, slots, send_sems, recv_sems in (
@@ -188,10 +213,14 @@
         for slot in range(1, count):
             gram = gram + slots[slot]
 
-    upper, inverse = eliminate(unpack(gram))
-    triangle[...] = upper * (1.0 / math.sqrt(rows * n_users))
+    gram_out[...] = gram
+
+
+def finish(scale, local, gram, basis, triangle):
+    upper, inverse = eliminate(unpack(gram[...]))
+    triangle[...] = upper * scale
     basis[...] = jnp.dot(
-        inverse, local, precision=HIGHEST, preferred_element_type=jnp.float32
+        inverse, local[...], precision=HIGHEST, preferred_element_type=jnp.float32
     )
 
 
@@ -202,11 +231,11 @@
     share = rows // n_hours
     dma = lambda count: pltpu.SemaphoreType.DMA((count,))
     vmem = pl.BlockSpec(memory_space=pltpu.VMEM)
-    basis, triangle = pl.pallas_call(
+    local, gram = pl.pallas_call(
         functools.partial(kernel, n_users, n_hours),
         out_shape=(
             jax.ShapeDtypeStruct((k, share), jnp.float32),
-            jax.ShapeDtypeStruct((k, k), jnp.float32),
+            jax.ShapeDtypeStruct((k // 2, 2 * k), jnp.float32),
         ),
         in_specs=[pl.BlockSpec(memory_space=pl.ANY), vmem, vmem, vmem],
         out_specs=(vmem, vmem),
@@ -214,6 +243,7 @@
             pltpu.VMEM((n_hours, share, width), jnp.bfloat16),
             pltpu.VMEM((2, k, EDGE), jnp.bfloat16),
             pltpu.VMEM((TAPS * k, width), jnp.bfloat16),
+            pltpu.VMEM((TAPS * k, 2 * EDGE), jnp.bfloat16),
             pltpu.VMEM((TAPS, rows), jnp.float32),
             pltpu.VMEM((n_hours - 1, k, share), jnp.float32),
             pltpu.VMEM((n_hours - 1, k, share), jnp.float32),
@@ -229,6 +259,16 @@
         ),
         name="range_finder",
     )(activity, cohort[None, :], tap_table, sketch.T)
+    basis, triangle = pl.pallas_call(
+        functools.partial(finish, 1.0 / math.sqrt(rows * n_users)),
+        out_shape=(
+            jax.ShapeDtypeStruct((k, share), jnp.float32),
+            jax.ShapeDtypeStruct((k, k), jnp.float32),
+        ),
+        in_specs=[vmem, vmem],
+        out_specs=(vmem, vmem),
+        name="factor",
+    )(local, gram)
     return basis.T, triangle
 
 

time: 34.5 us -> 27.9 us (0.81)
  Pallas kernels: 30.7 us -> 27.2 us
  local copies, waits for them, and re-layouts: 2.94 us -> 0 us
    pallas_call x1, Pallas kernels: 30.7 us -> 23.5 us  [per_device(): pl.pallas_call(functools.partial(kernel, n_users, n_hours), out_shape=(ja...]
    pallas_call x0 -> x1, Pallas kernels: none -> 3.62 us  [per_device(): pl.pallas_call(functools.partial(finish, 1.0 / math.sqrt(rows * n_users))...]
    unnamed x2 -> x0, local copies, waits for them, and re-layouts: 2.94 us -> none
where the time goes in v2:
time: 27.9 us; the launch traced here: 27.8 us
  Pallas kernels  27.2 us (97%)
  between operations  0.64 us (2%)
    pallas_call x1, Pallas kernels, per_device(): pl.pallas_call(functools.partial(kernel, n_users, n_hours), out_shape=(ja...  23.5 us
    pallas_call x1, Pallas kernels, per_device(): pl.pallas_call(functools.partial(finish, 1.0 / math.sqrt(rows * n_users))...  3.62 us

profile of v2, /device:TPU:0, one launch (start us, length us, event | category | flops | bytes accessed | tf_op | source)
XLA Modules:
  0.0 27.8 jit_solution(7629099318016828905)
XLA Ops:
  0.6 23.5 %range_finder.1 = (f32[64,512]{1,0:T(8,128)}, f32[32,128]{1,0:T(8,128)}) custom-call(bf16[2048,2048]{1,0:T(8,128)(2,1)} %activity.1, s32[1,2048]{1,0:T(1,128)} %bitcast.4, f32[16,9]{1,0:T(8,128)} %table.1, bf16[64,2048]{1,0:T(8,128)(2,1)} %bitcast.3), custom_call_target="tpu_custom_call" | custom-call | tf_op jit(solution)/shard_map/range_finder/pallas_call | solution.py:234
  24.2 3.6 %factor.1 = (f32[64,512]{1,0:T(8,128)}, f32[64,64]{1,0:T(8,128)}) custom-call(f32[64,512]{1,0:T(8,128)} %get-tuple-element.6.local, f32[32,128]{1,0:T(8,128)} %get-tuple-element.7.gram), custom_call_target="tpu_custom_call" | custom-call | tf_op jit(solution)/shard_map/factor/pallas_call | solution.py:262

commit v3 on v2

--- a/solution.py
+++ b/solution.py
@@ -28,6 +28,14 @@
 def dot_nt(a, b, precision=None):
     return lax.dot_general(
         a, b, (((1,), (1,)), ((), ())), precision=precision, preferred_element_type=jnp.float32
+    )
+
+
+def multiply(shifted, block, slot):
+    share = block.shape[1]
+    half = share // 2
+    return jnp.concatenate(
+        [dot_nt(shifted[...], block[slot, pl.ds(first, half), :]) for first in (0, half)], axis=1
     )
 
 
@@ -102,6 +110,23 @@
         pl.semaphore_signal(
             barrier, inc=1, device_id={"users": (users + step) % n_users}, device_id_type=MESH
         )
+    cohorts = table.shape[0]
+    onehot = (
+        lax.broadcasted_iota(jnp.int32, (cohorts, rows), 0) == cohort[...]
+    ).astype(jnp.float32)
+    taps[...] = lax.dot_general(
+        table[...], onehot, (((0,), (0,)), ((), ())),
+        precision=HIGHEST, preferred_element_type=jnp.float32,
+    )
+
+    middle = sketch[...].astype(jnp.float32)
+    blank = jnp.zeros((k, EDGE), jnp.float32)
+    turned = jnp.concatenate([blank, middle, blank], axis=1)
+    for step in range(TAPS):
+        shift = (step - REACH) % turned.shape[1]
+        moved = turned if shift == 0 else pltpu.roll(turned, shift, 1)
+        shifted[pl.ds(step * k, k), :] = moved[:, EDGE : EDGE + width].astype(jnp.bfloat16)
+
     pl.semaphore_wait(barrier, n_hours - 1 + n_users - 1)
 
     to_right = pltpu.make_async_remote_copy(
@@ -123,25 +148,8 @@
     to_right.start()
     to_left.start()
 
-    cohorts = table.shape[0]
-    onehot = (
-        lax.broadcasted_iota(jnp.int32, (cohorts, rows), 0) == cohort[...]
-    ).astype(jnp.float32)
-    taps[...] = lax.dot_general(
-        table[...], onehot, (((0,), (0,)), ((), ())),
-        precision=HIGHEST, preferred_element_type=jnp.float32,
-    )
-
-    middle = sketch[...].astype(jnp.float32)
-    blank = jnp.zeros((k, EDGE), jnp.float32)
-    turned = jnp.concatenate([blank, middle, blank], axis=1)
-    for step in range(TAPS):
-        shift = (step - REACH) % turned.shape[1]
-        moved = turned if shift == 0 else pltpu.roll(turned, shift, 1)
-        shifted[pl.ds(step * k, k), :] = moved[:, EDGE : EDGE + width].astype(jnp.bfloat16)
-
     loads[0].wait()
-    product = dot_nt(shifted[...], block[order[0]])
+    product = multiply(shifted, block, order[0])
 
     to_right.wait()
     to_left.wait()
@@ -164,7 +172,7 @@
         start = pl.multiple_of(flip(hours, mask) * share, share)
         if mask != order[0]:
             load.wait()
-            product = dot_nt(shifted[...], block[mask])
+            product = multiply(shifted, block, mask)
         total = taps[pl.ds(0, 1), pl.ds(start, share)] * product[:k]
         for step in range(1, TAPS):
             total += (

time: 27.9 us -> 26.8 us (0.961)
  Pallas kernels: 27.2 us -> 26 us
    pallas_call x1, Pallas kernels: 23.5 us -> 22.4 us  [per_device(): pl.pallas_call(functools.partial(kernel, n_users, n_hours), out_shape=(ja...]
where the time goes in v3:
time: 26.8 us; the launch traced here: 26.6 us
  Pallas kernels  26 us (97%)
  between operations  0.64 us (2%)
    pallas_call x1, Pallas kernels, per_device(): pl.pallas_call(functools.partial(kernel, n_users, n_hours), out_shape=(ja...  22.4 us
    pallas_call x1, Pallas kernels, per_device(): pl.pallas_call(functools.partial(finish, 1.0 / math.sqrt(rows * n_users))...  3.61 us

profile of v3, /device:TPU:0, one launch (start us, length us, event | category | flops | bytes accessed | tf_op | source)
XLA Modules:
  0.0 26.6 jit_solution(6657750766472567889)
XLA Ops:
  0.6 22.4 %range_finder.1 = (f32[64,512]{1,0:T(8,128)}, f32[32,128]{1,0:T(8,128)}) custom-call(bf16[2048,2048]{1,0:T(8,128)(2,1)} %activity.1, s32[1,2048]{1,0:T(1,128)} %bitcast.4, f32[16,9]{1,0:T(8,128)} %table.1, bf16[64,2048]{1,0:T(8,128)(2,1)} %bitcast.3), custom_call_target="tpu_custom_call" | custom-call | tf_op jit(solution)/shard_map/range_finder/pallas_call | solution.py:242
  23.0 3.6 %factor.1 = (f32[64,512]{1,0:T(8,128)}, f32[64,64]{1,0:T(8,128)}) custom-call(f32[64,512]{1,0:T(8,128)} %get-tuple-element.6.local, f32[32,128]{1,0:T(8,128)} %get-tuple-element.7.gram), custom_call_target="tpu_custom_call" | custom-call | tf_op jit(solution)/shard_map/factor/pallas_call | solution.py:270

commit v4 on v3

--- a/solution.py
+++ b/solution.py
@@ -82,7 +82,7 @@
 
 def kernel(
     n_users, n_hours, activity, cohort, table, sketch, local_out, gram_out,
-    block, edge, shifted, ends, taps, send, recv, gram_h, gram_u,
+    block, edge, shifted, ends, taps, send, recv, send_far, recv_far, gram_h, gram_u,
     load_sem, edge_send, edge_recv, part_send, part_recv, gh_send, gh_recv, gu_send, gu_recv,
 ):
     users = lax.axis_index("users")
@@ -181,13 +181,16 @@
         bit = 1
         while mask + bit < n_hours and (mask == 0 or bit < mask & -mask):
             copies[mask + bit].wait()
-            total += recv[mask + bit - 1]
+            arrived = recv if bit == 1 else recv_far
+            total += arrived[mask + bit - 1].astype(jnp.float32)
             bit *= 2
         if mask:
-            send[mask - 1] = total
+            near = mask % 2 == 1
+            source, target = (send, recv) if near else (send_far, recv_far)
+            source[mask - 1] = total.astype(source.dtype)
             copies[mask] = pltpu.make_async_remote_copy(
-                src_ref=send.at[mask - 1],
-                dst_ref=recv.at[mask - 1],
+                src_ref=source.at[mask - 1],
+                dst_ref=target.at[mask - 1],
                 send_sem=part_send.at[mask - 1],
                 recv_sem=part_recv.at[mask - 1],
                 device_id={"hours": flip(hours, mask & -mask)},
@@ -255,6 +258,8 @@
             pltpu.VMEM((TAPS, rows), jnp.float32),
             pltpu.VMEM((n_hours - 1, k, share), jnp.float32),
             pltpu.VMEM((n_hours - 1, k, share), jnp.float32),
+            pltpu.VMEM((n_hours - 1, k, share), jnp.bfloat16),
+            pltpu.VMEM((n_hours - 1, k, share), jnp.bfloat16),
             pltpu.VMEM((n_hours, k // 2, 2 * k), jnp.float32),
             pltpu.VMEM((n_users, k // 2, 2 * k), jnp.float32),
             dma(n_hours), dma(2), dma(2),

time: 26.8 us -> 25.4 us (0.948)
  Pallas kernels: 26 us -> 24.6 us
    pallas_call x1, Pallas kernels: 22.4 us -> 21 us  [per_device(): pl.pallas_call(functools.partial(kernel, n_users, n_hours), out_shape=(ja...]
where the time goes in v4:
time: 25.4 us; the launch traced here: 25.2 us
  Pallas kernels  24.6 us (97%)
  between operations  0.64 us (3%)
    pallas_call x1, Pallas kernels, per_device(): pl.pallas_call(functools.partial(kernel, n_users, n_hours), out_shape=(ja...  21 us
    pallas_call x1, Pallas kernels, per_device(): pl.pallas_call(functools.partial(finish, 1.0 / math.sqrt(rows * n_users))...  3.62 us

profile of v4, /device:TPU:0, one launch (start us, length us, event | category | flops | bytes accessed | tf_op | source)
XLA Modules:
  0.0 25.2 jit_solution(6288744670613447879)
XLA Ops:
  0.6 21.0 %range_finder.1 = (f32[64,512]{1,0:T(8,128)}, f32[32,128]{1,0:T(8,128)}) custom-call(bf16[2048,2048]{1,0:T(8,128)(2,1)} %activity.1, s32[1,2048]{1,0:T(1,128)} %bitcast.4, f32[16,9]{1,0:T(8,128)} %table.1, bf16[64,2048]{1,0:T(8,128)(2,1)} %bitcast.3), custom_call_target="tpu_custom_call" | custom-call | tf_op jit(solution)/shard_map/range_finder/pallas_call | solution.py:245
  21.6 3.6 %factor.1 = (f32[64,512]{1,0:T(8,128)}, f32[64,64]{1,0:T(8,128)}) custom-call(f32[64,512]{1,0:T(8,128)} %get-tuple-element.6.local, f32[32,128]{1,0:T(8,128)} %get-tuple-element.7.gram), custom_call_target="tpu_custom_call" | custom-call | tf_op jit(solution)/shard_map/factor/pallas_call | solution.py:275

commit v5 on v4

--- a/solution.py
+++ b/solution.py
@@ -230,8 +230,15 @@
 def finish(scale, local, gram, basis, triangle):
     upper, inverse = eliminate(unpack(gram[...]))
     triangle[...] = upper * scale
+    high = inverse.astype(jnp.bfloat16)
+    rest = (inverse - high.astype(jnp.float32)).astype(jnp.bfloat16)
+    values = local[...]
+    main = values.astype(jnp.bfloat16)
+    minor = (values - main.astype(jnp.float32)).astype(jnp.bfloat16)
     basis[...] = jnp.dot(
-        inverse, local[...], precision=HIGHEST, preferred_element_type=jnp.float32
+        jnp.concatenate([high, rest, high], axis=1),
+        jnp.concatenate([main, main, minor], axis=0),
+        preferred_element_type=jnp.float32,
     )
 
 

time: 25.4 us -> 25.3 us (level)
  no operation moved by 1% of the time
where the time goes in v5:
time: 25.3 us; the launch traced here: 25.2 us
  Pallas kernels  24.5 us (97%)
  between operations  0.64 us (3%)
    pallas_call x1, Pallas kernels, per_device(): pl.pallas_call(functools.partial(kernel, n_users, n_hours), out_shape=(ja...  21 us
    pallas_call x1, Pallas kernels, per_device(): pl.pallas_call(functools.partial(finish, 1.0 / math.sqrt(rows * n_users))...  3.57 us

profile of v5, /device:TPU:0, one launch (start us, length us, event | category | flops | bytes accessed | tf_op | source)
XLA Modules:
  0.0 25.2 jit_solution(10738930272815901066)
XLA Ops:
  0.6 21.0 %range_finder.1 = (f32[64,512]{1,0:T(8,128)}, f32[32,128]{1,0:T(8,128)}) custom-call(bf16[2048,2048]{1,0:T(8,128)(2,1)} %activity.1, s32[1,2048]{1,0:T(1,128)} %bitcast.4, f32[16,9]{1,0:T(8,128)} %table.1, bf16[64,2048]{1,0:T(8,128)(2,1)} %bitcast.3), custom_call_target="tpu_custom_call" | custom-call | tf_op jit(solution)/shard_map/range_finder/pallas_call | solution.py:252
  21.6 3.6 %factor.1 = (f32[64,512]{1,0:T(8,128)}, f32[64,64]{1,0:T(8,128)}) custom-call(f32[64,512]{1,0:T(8,128)} %get-tuple-element.6.local, f32[32,128]{1,0:T(8,128)} %get-tuple-element.7.gram), custom_call_target="tpu_custom_call" | custom-call | tf_op jit(solution)/shard_map/factor/pallas_call | solution.py:282
